TPU v7x, 32 devices: a whole 2x2x4 slice. The times are simulated.
32 devices in a mesh: bead: 8 (over z, core), space: 4 (over y, x).
Axes of the slice: x: 2, y: 2, z: 4, core: 2. Of those that a mesh axis runs over, the one named last changes fastest.
Arguments:
- positions: float32 [3, 32, 16384], P(None, 'bead', 'space'), may hold values from -0.12 to 2.12
- momenta: float32 [3, 32, 16384], P(None, 'bead', 'space'), may hold values from -6 to 6
- atom_types: int32 [16384], P('space'), may hold values from 0 to 3
- neighbours: int32 [128, 5], P('space'), may hold values from 0 to 127, as said below
- thermal_noise: float32 [2, 3, 32, 16384], P(None, None, 'bead', 'space'), may hold values from -6 to 6
Outputs:
- positions_out: float32 [3, 32, 16384], P(None, 'bead', 'space')
- momenta_out: float32 [3, 32, 16384], P(None, 'bead', 'space')
Inputs may be any that keep to these rules, and one draw needn't show every extreme that they name: `neighbours`: the row of block b holds 5 different blocks within 4 blocks of b, b itself and one block exactly 4 away among them.
All inputs are finite; a program needn't handle non-finite values.
Results may differ from a plain program's by a relative error of at most 0.0003.
Values sent between devices are 32-bit elements; how exact they have to be, the bound alone decides.
No kernel may reach another device: no remote copies, remote signals or barrier semaphores. Data moves between devices by JAX's collectives and lax.ppermute only.
A program may use at most 64 MiB of HBM per device.

v0:
```python
import functools
import math

import jax
import jax.numpy as jnp
import numpy as np
from jax import lax
from jax.experimental import pallas as pl
from jax.experimental.pallas import tpu as pltpu
from jax.sharding import PartitionSpec as P

BLOCK = 128
HALO = 4

half_step = 0.025
time_step = 0.05
chain_freq = 12.0
thermal = 0.375
centroid_friction = 1.0
screening = 4.0
softening = 0.09
CHARGES = (1.0, -1.0, 0.6, -1.4)
MASSES = (1.0, 2.0, 3.0, 4.0)

PAIR_ROWS = 24
PAIR_PAD = 32
SUM_ROWS = 16
QUAD = 4
PASS = 32
FRAME = 8
f32 = jnp.float32
bf16 = jnp.bfloat16


def mode_constants(bead_total):
    j = np.arange(bead_total)[:, None]
    k = np.arange(bead_total)[None, :]
    half = bead_total // 2
    phase = 2.0 * np.pi * ((j * k) % bead_total) / bead_total
    plain = 1.0 / math.sqrt(bead_total)
    paired = math.sqrt(2.0 / bead_total)
    matrix = np.where(
        k == 0,
        plain,
        np.where(
            k < half,
            paired * np.cos(phase),
            np.where(k == half, plain * np.cos(phase), paired * np.sin(phase)),
        ),
    )
    modes = np.arange(bead_total)
    frequency = 2.0 * chain_freq * np.sin(np.pi * modes / bead_total)
    angle = frequency * time_step
    ratio = np.where(modes == 0, time_step, np.sin(angle) / np.where(modes == 0, 1.0, frequency))
    friction = np.where(modes == 0, centroid_friction, 2.0 * frequency)
    damping = np.exp(-friction * time_step)
    kick = np.sqrt(1.0 - damping * damping)
    tables = np.stack([np.cos(angle), ratio, frequency * np.sin(angle), damping, kick])
    tables = np.broadcast_to(tables[:, :, None], tables.shape + (BLOCK,))
    return matrix.astype(np.float32), np.ascontiguousarray(tables).astype(np.float32)


def split3(v):
    one = v.astype(bf16).astype(f32)
    rest = v - one
    two = rest.astype(bf16).astype(f32)
    three = (rest - two).astype(bf16).astype(f32)
    return one, two, three


def pair_rows(coords, norm, own):
    rows = []
    for v in coords:
        one, two, three = split3(v)
        if own:
            one, two, three = -2.0 * one, -2.0 * two, -2.0 * three
            rows += [one, one, two, two, one, three]
        else:
            rows += [one, two, one, two, three, one]
    ones = [jnp.ones_like(norm)] * 3
    norms = list(split3(norm))
    return rows + (norms + ones if own else ones + norms)


def weigh_plain(square):
    inverse = lax.rsqrt(square)
    decay = jnp.exp2(square * inverse * (-1.0 / (screening * math.log(2.0))))
    return decay * ((inverse * inverse) * (inverse + 1.0 / screening))


def weigh_log(square):
    half = lax.log(square) * (-0.5 / math.log(2.0))
    inverse = jnp.exp2(half)
    decay = jnp.exp2((square * inverse * (-1.0 / (screening * math.log(2.0))) + half) + half)
    return decay * (inverse + 1.0 / screening)


def weigh_newton(square):
    coarse = lax.rsqrt(square.astype(bf16)).astype(f32)
    twice = coarse * (3.0 - square * (coarse * coarse))
    decay = jnp.exp2(square * twice * (-0.5 / (screening * math.log(2.0))))
    return decay * ((twice * twice) * (0.125 * twice + 0.25 / screening))


def whole_quads(beads):
    return -(-beads // QUAD) * QUAD


def add_forces(weigh, blocks, margin, listed, offset_ref, charge_ref, coord_ref, scratch):
    rows_ref, sums_ref, far_ref, heavy_ref, near_ref, total_ref, force_ref, *buffers = scratch
    square_refs, weight_refs = buffers[:2], buffers[2:]
    beads = coord_ref.shape[1]
    pairs = beads // 2
    frame = min(FRAME, blocks)
    width = frame + 2 * margin
    middle = margin + (frame - 1) / 2.0
    at_once = max(1, 8 // beads)
    lines = at_once * beads
    units = blocks * pairs

    def put(ref, k, value):
        ref[k * lines:(k + 1) * lines, :] = value

    def centred(block, place):
        spans = [pl.ds(pl.multiple_of((block + i) * BLOCK, BLOCK), BLOCK) for i in range(at_once)]
        coords = [
            jnp.concatenate([coord_ref[c, :, lanes] for lanes in spans], axis=0) - 1.0 for c in range(3)
        ]
        shift = jnp.concatenate(
            [jnp.full((beads, BLOCK), 1.0, f32) * ((place + i).astype(f32) - middle) for i in range(at_once)], axis=0
        )
        coords[0] = coords[0] + shift
        norm = coords[0] * coords[0] + coords[1] * coords[1] + coords[2] * coords[2]
        charge = jnp.concatenate(
            [jnp.broadcast_to(charge_ref[:, lanes], (beads, BLOCK)) for lanes in spans], axis=0
        )
        return coords, norm, charge

    nothing = jnp.zeros((lines, BLOCK), f32)
    for k in range(PAIR_ROWS, PAIR_PAD):
        put(rows_ref, k, nothing)
    for k in range(12, SUM_ROWS):
        put(sums_ref, k, nothing)
    blank = jnp.zeros((PAIR_PAD, BLOCK), f32)

    def one_frame(at_frame, carry):
        first = at_frame * frame

        def one_table(step, inner):
            place = step * at_once
            coords, norm, charge = centred(first + place, place)
            for k, row in enumerate(pair_rows(coords, norm, False)):
                put(rows_ref, k, row)
            for c, v in enumerate([charge] + [charge * x for x in coords]):
                for level, part in enumerate(split3(v)):
                    put(sums_ref, level * 4 + c, part)
            for i in range(at_once):
                at = at_frame * width + place + i
                for quad in range(beads // QUAD):
                    low = i * beads + quad * QUAD
                    four = jnp.concatenate(
                        [rows_ref[pl.ds(low + j, PAIR_PAD, stride=lines), :] for j in range(QUAD)], axis=0
                    )
                    far_ref[at, quad] = jnp.transpose(four).astype(bf16)
                    for half in range(2):
                        heavy_ref[at, 2 * quad + half] = jnp.concatenate(
                            [
                                sums_ref[pl.ds(low + 2 * half + j, SUM_ROWS, stride=lines), :]
                                for j in range(2)
                            ],
                            axis=0,
                        ).astype(bf16)
            return inner

        lax.fori_loop(0, width // at_once, one_table, 0)

        def one_own(step, inner):
            block = step * at_once
            coords, norm, _ = centred(first + margin + block, block + margin)
            for k, row in enumerate(pair_rows(coords, norm + softening, True)):
                put(rows_ref, k, row)
            for i in range(at_once):
                for pair in range(pairs):
                    columns = []
                    for j in range(2):
                        own = rows_ref[pl.ds(i * beads + 2 * pair + j, PAIR_PAD, stride=lines), :]
                        spot = 2 * pair % QUAD + j
                        columns.append(
                            jnp.concatenate([own if k == spot else blank for k in range(QUAD)], axis=0)
                        )
                    near_ref[(first + block + i) * pairs + pair] = jnp.concatenate(columns, axis=1).astype(bf16)
            return inner

        lax.fori_loop(0, frame // at_once, one_own, 0)
        return carry

    lax.fori_loop(0, blocks // frame, one_frame, 0)

    def places(unit):
        block = unit // pairs
        at_frame = block // frame
        base = at_frame * width + block - at_frame * frame + margin
        return [base + offset_ref[block * listed + m] for m in range(listed)], unit - block * pairs

    def squares(unit, out):
        ats, pair = places(unit)
        far = jnp.concatenate([far_ref[at, pair // (QUAD // 2)] for at in ats], axis=0)
        out[...] = jnp.dot(far, near_ref[unit], preferred_element_type=f32)

    def weights(square_ref, out):
        for m in range(listed):
            for low in range(0, BLOCK, PASS):
                weight = weigh(square_ref[m * BLOCK + low:m * BLOCK + low + PASS, :])
                high = weight.astype(bf16)
                row = 2 * m * BLOCK + low
                out[row:row + PASS, :] = high
                out[row + BLOCK:row + BLOCK + PASS, :] = (weight - high.astype(f32)).astype(bf16)

    def sums(unit, weight_ref, slot):
        ats, pair = places(unit)
        tables = [heavy_ref[at, pair] for at in ats]
        total = jnp.dot(
            jnp.concatenate([t for table in tables for t in (table, table)], axis=1),
            weight_ref[...], preferred_element_type=f32,
        )
        for i in range(2):
            cols = slice(i * BLOCK, (i + 1) * BLOCK)
            row = i * SUM_ROWS
            spot = pl.ds(pl.multiple_of((2 * slot + i) * 8, 8), 8)
            total_ref[spot, :] = total[row:row + 8, cols] + total[row + 8:row + 16, cols]

    squares(0, square_refs[0])

    def two_units(step, carry):
        unit = 2 * step
        squares(unit + 1, square_refs[1])
        weights(square_refs[0], weight_refs[0])
        sums(jnp.maximum(unit - 1, 0), weight_refs[1], jnp.where(unit == 0, units, unit - 1))
        squares(jnp.minimum(unit + 2, units - 1), square_refs[0])
        weights(square_refs[1], weight_refs[1])
        sums(unit, weight_refs[0], unit)
        return carry

    lax.fori_loop(0, units // 2, two_units, 0)
    sums(units - 1, weight_refs[1], units - 1)

    def one_block(block, carry):
        at_frame = block // frame
        place = block - at_frame * frame + margin
        lanes = pl.ds(pl.multiple_of((block + margin) * BLOCK, BLOCK), BLOCK)
        coords = [coord_ref[c, :, lanes] - 1.0 for c in range(3)]
        coords[0] = coords[0] + (place.astype(f32) - middle)
        charge = jnp.broadcast_to(charge_ref[:, lanes], coords[0].shape)

        def summed(c):
            return (
                total_ref[pl.ds(block * beads * 8 + c, beads, stride=8), :]
                + total_ref[pl.ds(block * beads * 8 + c + 4, beads, stride=8), :]
            )

        near = summed(0)
        own = pl.ds(pl.multiple_of(block * BLOCK, BLOCK), BLOCK)
        for c in range(3):
            force_ref[c, :, own] = charge * (coords[c] * near - summed(c + 1))
        return carry

    lax.fori_loop(0, blocks, one_block, 0)


def force_scratch(local, blocks, margin, listed):
    beads = whole_quads(local)
    frame = min(FRAME, blocks)
    tables = (frame + 2 * margin) * (blocks // frame)
    lines = max(8, beads)
    units = blocks * beads // 2
    return [
        pltpu.VMEM((3, beads, (blocks + 2 * margin) * BLOCK), f32),
        pltpu.VMEM((PAIR_PAD * lines, BLOCK), f32),
        pltpu.VMEM((SUM_ROWS * lines, BLOCK), f32),
        pltpu.VMEM((tables, beads // QUAD, BLOCK, QUAD * PAIR_PAD), bf16),
        pltpu.VMEM((tables, beads // 2, 2 * SUM_ROWS, BLOCK), bf16),
        pltpu.VMEM((units, QUAD * PAIR_PAD, 2 * BLOCK), bf16),
        pltpu.VMEM(((units + 1) * 16, BLOCK), f32),
        pltpu.VMEM((3, beads, blocks * BLOCK), f32),
        pltpu.VMEM((listed * BLOCK, 2 * BLOCK), f32),
        pltpu.VMEM((listed * BLOCK, 2 * BLOCK), f32),
        pltpu.VMEM((2 * listed * BLOCK, 2 * BLOCK), bf16),
        pltpu.VMEM((2 * listed * BLOCK, 2 * BLOCK), bf16),
    ]


def call(kernel, args, smem_count, shapes, scratch, work):
    vmem = pl.BlockSpec(memory_space=pltpu.VMEM)
    smem = pl.BlockSpec(memory_space=pltpu.SMEM)
    return pl.pallas_call(
        kernel,
        out_shape=[jax.ShapeDtypeStruct(shape, f32) for shape in shapes],
        in_specs=[smem] * smem_count + [vmem] * (len(args) - smem_count),
        out_specs=[vmem] * len(shapes),
        scratch_shapes=scratch,
        compiler_params=pltpu.CompilerParams(vmem_limit_bytes=40 * 1024 * 1024),
        cost_estimate=pl.CostEstimate(
            flops=20 * work + 1024, bytes_accessed=4 * 1024 * 1024, transcendentals=2 * work
        ),
    )(*args)


def row_of(c, block, blocks, local):
    return (c * blocks + block) * local


def unpack_beads(source, base, blocks, local, target, offset):
    for c in range(3):
        for block in range(blocks):
            row = row_of(base + c, block, blocks, local)
            lane = offset + block * BLOCK
            for group in range(source.shape[0]):
                target[c, group * local:(group + 1) * local, lane:lane + BLOCK] = source[group, row:row + local, :]


def pack_beads(value, c, blocks, local, target):
    for block in range(blocks):
        row = row_of(c, block, blocks, local)
        for group in range(target.shape[0]):
            target[group, row:row + local, :] = value[
                group * local:(group + 1) * local, block * BLOCK:(block + 1) * BLOCK
            ]


FORCE = 6


def clear(coord_ref, local):
    if coord_ref.shape[1] != local:
        coord_ref[...] = jnp.zeros(coord_ref.shape, f32)


def first_kernel(
    shares, margin, listed, offset_ref, charge_ref, x_ref, message_ref, p_ref, pout_ref, coord_ref, *scratch
):
    _, local, atoms = x_ref.shape
    blocks = atoms // BLOCK
    each = blocks // shares
    edge = margin * BLOCK
    clear(coord_ref, local)
    for c in range(3):
        coord_ref[c, :local, 0:atoms] = x_ref[c]
        for part in range(2):
            coord_ref[c, :local, atoms + part * edge:atoms + (part + 1) * edge] = message_ref[3 * part + c]
    add_forces(weigh_log, blocks, margin, listed, offset_ref, charge_ref, coord_ref, scratch)
    force_ref = scratch[FORCE]
    for c in range(3):
        for block in range(blocks):
            lanes = slice(block * BLOCK, (block + 1) * BLOCK)
            at = block * BLOCK + edge
            if at < atoms:
                moment = p_ref[c, :, at:at + BLOCK]
            else:
                moment = message_ref[6 + c, :, at - atoms:at - atoms + BLOCK]
            row = row_of(c, block % each, each, local)
            pout_ref[block // each, row:row + local, :] = moment + half_step * force_ref[c, :local, lanes]


def last_kernel(
    margin, listed, offset_ref, charge_ref, both_ref, message_ref, xout_ref, pout_ref, coord_ref, *scratch
):
    shares = both_ref.shape[0]
    _, local, atoms = xout_ref.shape
    blocks = atoms // BLOCK
    each = blocks // shares
    edge = margin * BLOCK

    def taken(c, block):
        row = row_of(c, block % each, each, local)
        return both_ref[block // each, row:row + local, :]

    clear(coord_ref, local)
    for c in range(3):
        for part in range(2):
            coord_ref[c, :local, part * edge:(part + 1) * edge] = message_ref[3 * part + c]
        for block in range(blocks):
            at = 2 * edge + block * BLOCK
            coord_ref[c, :local, at:at + BLOCK] = taken(c, block)
        xout_ref[c] = coord_ref[c, :local, edge:edge + atoms]
    add_forces(weigh_newton, blocks, margin, listed, offset_ref, charge_ref, coord_ref, scratch)
    force_ref = scratch[FORCE]
    for c in range(3):
        for block in range(blocks):
            lanes = slice(block * BLOCK, (block + 1) * BLOCK)
            moment = message_ref[6 + c, :, lanes] if block < margin else taken(3 + c, block - margin)
            pout_ref[c, :, lanes] = moment + half_step * force_ref[c, :local, lanes]


def thermostat(coords, moments, noises, mass_ref, matrix_ref, matrix_t_ref, table_ref, store):
    beads, width = moments[0].shape
    cosine, ratio, stiffness, damping, kick = [
        jnp.concatenate([table_ref[i]] * (width // BLOCK), axis=1) for i in range(5)
    ]
    mass = jnp.broadcast_to(mass_ref[...], (beads, width))
    spread = kick * jnp.sqrt(thermal * mass)
    drift = ratio / mass
    stiff = stiffness * mass
    multiply = functools.partial(jnp.dot, precision=lax.Precision.HIGHEST, preferred_element_type=f32)
    for c in range(3):
        mode_x = multiply(matrix_t_ref[...], coords[c])
        mode_p = damping * multiply(matrix_t_ref[...], moments[c]) + spread * noises[c]
        store(
            c,
            multiply(matrix_ref[...], cosine * mode_x + drift * mode_p),
            multiply(matrix_ref[...], cosine * mode_p - stiff * mode_x),
        )


def modes_kernel(
    blocks, noise_base, rest_ref, p_ref, mass_ref, matrix_ref, matrix_t_ref, table_ref,
    xout_ref, pout_ref, coord_ref, moment_ref, noise_ref,
):
    local = p_ref.shape[1] // (3 * blocks)
    unpack_beads(rest_ref, 0, blocks, local, coord_ref, 0)
    unpack_beads(p_ref, 0, blocks, local, moment_ref, 0)
    unpack_beads(rest_ref, noise_base, blocks, local, noise_ref, 0)

    def store(c, x, p):
        pack_beads(x, c, blocks, local, xout_ref)
        pack_beads(p, c, blocks, local, pout_ref)

    thermostat(
        *[[ref[c] for c in range(3)] for ref in (coord_ref, moment_ref, noise_ref)],
        mass_ref, matrix_ref, matrix_t_ref, table_ref, store,
    )


def middle_kernel(hops, blocks, listed, noise_base, joined, offset_ref, charge_ref, *refs):
    parts = 2 * hops + 1
    x_refs = refs[:parts]
    p_ref, noise_ref, mass_ref, matrix_ref, matrix_t_ref, table_ref = refs[parts:parts + 6]
    outs = refs[parts + 6:parts + (7 if joined else 8)]
    coord_ref, *scratch = refs[parts + len(outs) + 6:]
    beads = coord_ref.shape[1]
    local = beads // p_ref.shape[0]
    width = blocks * BLOCK
    for part in range(parts):
        unpack_beads(x_refs[part], 0, blocks, local, coord_ref, part * width)
    add_forces(weigh_plain, blocks, hops * blocks, listed, offset_ref, charge_ref, coord_ref, scratch)
    force_ref = scratch[FORCE]
    unpack_beads(p_ref, 0, blocks, local, coord_ref, 0)
    unpack_beads(noise_ref, noise_base, blocks, local, coord_ref, (parts - 1) * width)

    def share(c, part):
        return coord_ref[c, :, part * width:(part + 1) * width]

    def store(c, x, p):
        pack_beads(x, c, blocks, local, outs[0])
        if joined:
            pack_beads(p, 3 + c, blocks, local, outs[0])
        else:
            pack_beads(p, c, blocks, local, outs[1])

    thermostat(
        [share(c, hops) for c in range(3)],
        [share(c, 0) + 2.0 * half_step * force_ref[c] for c in range(3)],
        [share(c, parts - 1) for c in range(3)],
        mass_ref, matrix_ref, matrix_t_ref, table_ref, store,
    )


def fold(count):
    return [i // 2 if i % 2 == 0 else count - 1 - i // 2 for i in range(count)]


def exchange(pieces):
    order = fold(pieces.shape[0])
    group = [order.index(at) for at in range(len(order))]
    return lax.all_to_all(pieces, "bead", split_axis=0, concat_axis=0, axis_index_groups=[group], tiled=True)


def pack_shares(values):
    count = lax.axis_size("bead")
    lead, local, atoms = values.shape
    blocks = atoms // (count * BLOCK)
    pieces = values.reshape(lead, local, count, blocks, BLOCK).transpose(2, 0, 3, 1, 4)
    return pieces.reshape(count, lead * blocks * local, BLOCK)


def passed(values, step):
    count = lax.axis_size("space")
    return lax.ppermute(values, "space", [(i, (i + step) % count) for i in range(count)])


def window(values, hops):
    count = lax.axis_size("bead")
    domains = lax.axis_size("space")
    order = fold(count)
    device = {}
    for bead in range(count):
        for domain in range(domains):
            device[domain * count + order[bead]] = bead * domains + domain
    total = count * domains
    out = []
    for hop in range(-hops, hops + 1):
        if hop == 0:
            out.append(values)
        else:
            route = [(device[(at + hop) % total], device[at]) for at in range(total)]
            out.append(lax.ppermute(values, ("bead", "space"), route))
    return out


def body(positions, momenta, atom_types, neighbours, thermal_noise):
    count = lax.axis_size("bead")
    _, local, atoms = positions.shape
    beads = local * count
    domain = atoms // BLOCK
    blocks = domain // count
    share = blocks * BLOCK
    hops = -(-HALO // blocks)
    margin = hops * blocks
    edge = margin * BLOCK
    steps = thermal_noise.shape[0]
    listed = neighbours.shape[1]
    order = fold(count)

    charge = jnp.zeros(atom_types.shape, f32)
    mass = jnp.zeros(atom_types.shape, f32)
    for kind in range(4):
        charge = jnp.where(atom_types == kind, CHARGES[kind], charge)
        mass = jnp.where(atom_types == kind, MASSES[kind], mass)
    own = lax.axis_index("space") * domain + jnp.arange(domain, dtype=jnp.int32)
    offsets = jnp.clip(neighbours - own[:, None], -margin, margin)
    noises = thermal_noise.reshape(3 * steps, local, atoms)

    wide = jnp.stack([
        charge[:edge], charge[edge:2 * edge], mass[:edge],
        jnp.pad(offsets[:margin].astype(f32).reshape(-1), (0, edge - margin * listed)),
    ])
    message = passed(jnp.concatenate([
        positions[:, :, :edge], positions[:, :, edge:2 * edge], momenta[:, :, :edge], noises[:, :, :edge],
        jnp.broadcast_to(wide[:, None, :], (4, local, edge)),
    ], axis=0), -1)
    side = message[9 + 3 * steps:, 0]
    first_charge = jnp.concatenate([charge, side[0], side[1]])[None, :]
    moved_mass = jnp.concatenate([mass[edge:], side[2]])
    moved_offsets = jnp.concatenate([offsets[margin:].reshape(-1), side[3, :margin * listed].astype(jnp.int32)])
    rest = exchange(pack_shares(jnp.concatenate([
        jnp.concatenate([positions, noises], axis=0)[:, :, edge:],
        jnp.concatenate([message[:3], message[9:9 + 3 * steps]], axis=0),
    ], axis=2)))

    place = jnp.asarray(np.array(order, np.int32))[lax.axis_index("bead")]
    near_charge = lax.dynamic_slice_in_dim(first_charge, place * share, share + 2 * edge, axis=1)
    near_mass = lax.dynamic_slice_in_dim(moved_mass, place * share, share)[None, :]
    near_offsets = lax.dynamic_slice_in_dim(moved_offsets, place * blocks * listed, blocks * listed)

    matrix, tables = mode_constants(beads)
    at = np.concatenate([order.index(g) * local + np.arange(local) for g in range(count)])
    matrix = matrix[at][:, at]
    fixed = (near_mass, jnp.asarray(matrix), jnp.asarray(np.ascontiguousarray(matrix.T)), jnp.asarray(tables[:, at]))

    packed = (count, 3 * blocks * local, BLOCK)
    pairs = beads * blocks * listed * BLOCK * BLOCK
    (moment,) = call(
        functools.partial(first_kernel, count, margin, listed),
        (moved_offsets, first_charge, positions, message, momenta), 1, [packed],
        force_scratch(local, domain, margin, listed), pairs,
    )
    moment, rest = lax.optimization_barrier((moment, rest))
    coords, moment = call(
        functools.partial(modes_kernel, blocks, 3), (rest, exchange(moment)) + fixed, 0, [packed] * 2,
        [pltpu.VMEM((3, beads, share), f32)] * 3, 0,
    )
    for step in range(1, steps):
        joined = step == steps - 1
        out = call(
            functools.partial(middle_kernel, hops, blocks, listed, 3 * step + 3, joined),
            (near_offsets, near_charge) + tuple(window(coords, hops)) + (moment, rest) + fixed, 1,
            [(count, 6 * blocks * local, BLOCK)] if joined else [packed] * 2,
            force_scratch(beads, blocks, margin, listed), pairs,
        )
        if not joined:
            coords, moment = out
    both = exchange(out[0])

    def ends(low, c):
        pieces = both[low:low + hops, c * packed[1]:(c + 1) * packed[1]]
        return pieces.reshape(hops, 3, blocks, local, BLOCK).transpose(1, 3, 0, 2, 4).reshape(3, local, edge)

    message = passed(jnp.concatenate([
        ends(count - 2 * hops, 0), ends(count - hops, 0), ends(count - hops, 1),
        jnp.broadcast_to(charge[None, None, atoms - edge:], (1, local, edge)),
    ], axis=0), 1)
    last_charge = jnp.concatenate([message[9, 0], first_charge[0, :atoms + edge]])[None, :]
    return tuple(call(
        functools.partial(last_kernel, margin, listed), (offsets.reshape(-1), last_charge, both, message), 1,
        [(3, local, atoms)] * 2, force_scratch(local, domain, margin, listed), pairs,
    ))


def solution(mesh):
    placed = (
        P(None, "bead", "space"),
        P(None, "bead", "space"),
        P("space"),
        P("space", None),
        P(None, None, "bead", "space"),
    )
    return jax.shard_map(
        body,
        mesh=mesh,
        in_specs=placed,
        out_specs=(P(None, "bead", "space"), P(None, "bead", "space")),
        check_vma=False,
    )
```

profile of v0, /device:TPU:0, one launch (start us, length us, event | category | flops | bytes accessed | tf_op | source)
XLA Modules:
  0.0 178.0 jit_solution(2927089962656589864)
XLA Ops:
  0.6 0.0 copy-start.4
  0.6 0.8 fusion.2
  1.5 0.7 subtract_clamp_fusion
  2.2 0.1 copy.18
  2.3 0.1 reshape.63
  2.4 0.7 slice_dynamic-update-slice_fusion.3
  3.1 0.7 slice_dynamic-update-slice_fusion.2
  3.9 0.0 copy-done.4
  3.9 0.9 slice_dynamic-update-slice_fusion
  4.8 3.9 %collective-permute-start = (f32[19,4,512]{2,1,0:T(4,128)S(1)}, f32[19,4,512]{2,1,0:T(4,128)S(1)}, u32[]{:S(2)}, u32[]{:S(2)}) collective-permute-start(f32[19,4,512]{2,1,0:T(4,128)S(1)} %broadcast_dynamic-update-slice_fusion), channel_id=1, source_target_pairs={{0,3},{1,0},{2,1},{3,2},{4,7},{5,4},{6,5},{7,6},{8,11},{9,8},{10,9... | collective-permute-start | bytes 466952 | tf_op jit(solution)/shard_map/ppermute | solution.py:487
  8.7 3.3 %collective-permute-done.message_ref = f32[19,4,512]{2,1,0:T(4,128)S(1)} collective-permute-done((f32[19,4,512]{2,1,0:T(4,128)S(1)}, f32[19,4,512]{2,1,0:T(4,128)S(1)}, u32[]{:S(2)}, u32[]{:S(2)}) %collective-permute-start) | collective-permute-done | bytes 155680 | tf_op jit(solution)/shard_map/ppermute | solution.py:487
  12.0 0.0 copy-done
  12.0 1.1 fusion
  13.1 0.5 reshape.64
  13.6 1.2 copy.19
  14.9 4.9 %all-to-all-start = ((f32[8,144,128]{2,1,0:T(8,128)}), f32[8,144,128]{2,1,0:T(8,128)S(1)}, u32[]{:S(2)}, u32[]{:S(2)}) async-start(f32[8,144,128]{2,1,0:T(8,128)} %bitcast.12), calls=%async_computation | async-start | bytes 1179648 | tf_op jit(solution)/shard_map/all_to_all | solution.py:474
  19.8 0.1 slice.78
  19.8 0.1 copy.17
  19.9 0.1 reshape.61
  20.1 0.1 pad_add_fusion.offset_ref
  20.2 0.0 copy-start.5
  20.2 0.0 copy-start.2
  20.2 0.0 copy-start.3
  20.2 38.7 %shard_map.104 = f32[8,48,128]{2,1,0:T(8,128)} custom-call(s32[160]{0:T(256)S(1)} %pad_add_fusion.offset_ref, f32[1,5120]{1,0:T(1,128)S(1)} %bitcast.40, f32[3,4,4096]{2,1,0:T(4,128)S(1)} %copy-done, f32[19,4,512]{2,1,0:T(4,128)S(1)} %collective-permute-done.message_ref, f32[3,4,4096]{2,1,0:T(4,128)S(1)} %copy-done.4), custom_call_target="tpu_custom_call" | custom-call | flops 209716224 | bytes 4194304 | tf_op jit(solution)/shard_map/pallas_call | solution.py:295
  58.9 0.0 all-to-all-done.rest_ref.refs_4_
  58.9 5.1 %all-to-all-start.1 = ((f32[8,48,128]{2,1,0:T(8,128)}), f32[8,48,128]{2,1,0:T(8,128)S(1)}, u32[]{:S(2)}, u32[]{:S(2)}) async-start(f32[8,48,128]{2,1,0:T(8,128)} %shard_map.104), calls=%async_computation.1 | async-start | bytes 393216 | tf_op jit(solution)/shard_map/all_to_all | solution.py:474
  64.1 0.0 copy-done.5
  64.1 0.6 dynamic_slice.12
  65.3 0.1 fusion.5
  65.4 6.6 %all-to-all-done.1.p_ref = f32[8,48,128]{2,1,0:T(8,128)S(1)} async-done(((f32[8,48,128]{2,1,0:T(8,128)}), f32[8,48,128]{2,1,0:T(8,128)S(1)}, u32[]{:S(2)}, u32[]{:S(2)}) %all-to-all-start.1) | async-done | bytes 196640 | tf_op jit(solution)/shard_map/all_to_all | solution.py:474
  72.0 0.0 copy-done.2
  72.0 0.0 copy-done.3
  72.0 0.0 copy-done.1
  72.0 1.2 shard_map.105
  73.2 0.1 collective-permute-start.1
  73.3 3.1 %collective-permute-start.2 = (f32[8,48,128]{2,1,0:T(8,128)S(1)}, f32[8,48,128]{2,1,0:T(8,128)S(1)}, u32[]{:S(2)}, u32[]{:S(2)}) collective-permute-start(f32[8,48,128]{2,1,0:T(8,128)S(1)} %get-tuple-element.8.refs_1_), channel_id=1, source_target_pairs={{8,0},{16,8},{24,16},{28,24},{20,28},{12,20},{4,12},{1,4},{9,1},{1... | collective-permute-start | bytes 589832 | tf_op jit(solution)/shard_map/ppermute | solution.py:505
  77.1 0.1 dynamic-slice.3
  77.2 0.1 dynamic_slice.13.offset_ref
  77.3 2.5 %collective-permute-done.1.refs_0_ = f32[8,48,128]{2,1,0:T(8,128)S(1)} collective-permute-done((f32[8,48,128]{2,1,0:T(8,128)S(1)}, f32[8,48,128]{2,1,0:T(8,128)S(1)}, u32[]{:S(2)}, u32[]{:S(2)}) %collective-permute-start.1) | collective-permute-done | bytes 196640 | tf_op jit(solution)/shard_map/ppermute | solution.py:505
  79.7 0.7 collective-permute-done.2.refs_2_
  80.4 36.0 %shard_map.106 = f32[8,96,128]{2,1,0:T(8,128)} custom-call(s32[20]{0:T(128)S(1)} %dynamic_slice.13.offset_ref, f32[1,1536]{1,0:T(1,128)S(1)} %dynamic_slice.14.charge_ref, f32[8,48,128]{2,1,0:T(8,128)S(1)} %collective-permute-done.1.refs_0_, f32[8,48,128]{2,1,0:T(8,128)S(1)} %get-tuple-element.8.refs_1_, f32[8,48,128]{2,1,0:T(8,128)S(1)} %collective-permute-done.2.refs_2_, ...), custom_call_target="tpu_custom_call" | custom-call | flops 209716224 | bytes 4194304 | tf_op jit(solution)/shard_map/pallas_call | solution.py:295
  116.4 3.5 %all-to-all-start.2 = ((f32[8,96,128]{2,1,0:T(8,128)}), f32[8,96,128]{2,1,0:T(8,128)S(1)}, u32[]{:S(2)}, u32[]{:S(2)}) async-start(f32[8,96,128]{2,1,0:T(8,128)} %shard_map.106), calls=%async_computation.2 | async-start | bytes 786432 | tf_op jit(solution)/shard_map/all_to_all | solution.py:474
  119.9 0.1 copy.16
  119.9 0.1 reshape.60.offset_ref
  120.0 10.7 %all-to-all-done.2.both_ref = f32[8,96,128]{2,1,0:T(8,128)S(1)} async-done(((f32[8,96,128]{2,1,0:T(8,128)}), f32[8,96,128]{2,1,0:T(8,128)S(1)}, u32[]{:S(2)}, u32[]{:S(2)}) %all-to-all-start.2) | async-done | bytes 393248 | tf_op jit(solution)/shard_map/all_to_all | solution.py:474
  130.9 2.2 %collective-permute-start.3 = (f32[10,4,512]{2,1,0:T(4,128)S(1)}, f32[10,4,512]{2,1,0:T(4,128)S(1)}, u32[]{:S(2)}, u32[]{:S(2)}) collective-permute-start(f32[10,4,512]{2,1,0:T(4,128)S(1)} %pad_maximum_fusion.1), channel_id=1, source_target_pairs={{0,1},{1,2},{2,3},{3,0},{4,5},{5,6},{6,7},{7,4},{8,9},{9,10},{10,1... | collective-permute-start | bytes 245768 | tf_op jit(solution)/shard_map/ppermute | solution.py:487
  133.2 4.1 %collective-permute-done.3.message_ref = f32[10,4,512]{2,1,0:T(4,128)S(1)} collective-permute-done((f32[10,4,512]{2,1,0:T(4,128)S(1)}, f32[10,4,512]{2,1,0:T(4,128)S(1)}, u32[]{:S(2)}, u32[]{:S(2)}) %collective-permute-start.3) | collective-permute-done | bytes 81952 | tf_op jit(solution)/shard_map/ppermute | solution.py:487
  137.3 40.6 %shard_map.107 = (f32[3,4,4096]{2,1,0:T(4,128)}, f32[3,4,4096]{2,1,0:T(4,128)}) custom-call(s32[160]{0:T(256)S(1)} %reshape.60.offset_ref, f32[1,5120]{1,0:T(1,128)S(1)} %bitcast.42, f32[8,96,128]{2,1,0:T(8,128)S(1)} %all-to-all-done.2.both_ref, f32[10,4,512]{2,1,0:T(4,128)S(1)} %collective-permute-done.3.message_ref), custom_call_target="tpu_custom_call" | custom-call | flops 209716224 | bytes 4194304 | tf_op jit(solution)/shard_map/pallas_call | solution.py:295
  (32 shorter events, 0.3 us)
Async XLA Ops:
  0.6 3.2 %copy-start.4 = (f32[3,4,4096]{2,1,0:T(4,128)S(1)}, f32[3,4,4096]{2,1,0:T(4,128)}, u32[]{:S(2)}) copy-start(f32[3,4,4096]{2,1,0:T(4,128)} %p_ref.1) | copy-start | bytes 589828
  3.8 8.2 %copy-start = (f32[3,4,4096]{2,1,0:T(4,128)S(1)}, f32[3,4,4096]{2,1,0:T(4,128)}, u32[]{:S(2)}) copy-start(f32[3,4,4096]{2,1,0:T(4,128)} %x_ref.1) | copy-start | bytes 589828
  4.8 7.2 %collective-permute-start = (f32[19,4,512]{2,1,0:T(4,128)S(1)}, f32[19,4,512]{2,1,0:T(4,128)S(1)}, u32[]{:S(2)}, u32[]{:S(2)}) collective-permute-start(f32[19,4,512]{2,1,0:T(4,128)S(1)} %broadcast_dynamic-update-slice_fusion), channel_id=1, source_target_pairs={{0,3},{1,0},{2,1},{3,2},{4,7},{5,4},{6,5},{7,6},{8,11},{9,8},{10,9... | collective-permute-start | bytes 466952 | tf_op jit(solution)/shard_map/ppermute | solution.py:487
  14.9 44.1 %all-to-all-start = ((f32[8,144,128]{2,1,0:T(8,128)}), f32[8,144,128]{2,1,0:T(8,128)S(1)}, u32[]{:S(2)}, u32[]{:S(2)}) async-start(f32[8,144,128]{2,1,0:T(8,128)} %bitcast.12), calls=%async_computation | async-start | bytes 1179648 | tf_op jit(solution)/shard_map/all_to_all | solution.py:474
  20.2 43.9 %copy-start.5 = (s32[8]{0:T(128)S(1)}, s32[8]{0:T(128)}, u32[]{:S(2)}) copy-start(s32[8]{0:T(128)} %constant.64.clone) | copy-start | bytes 100
  20.2 51.8 %copy-start.2 = (f32[32,32]{1,0:T(8,128)S(1)}, f32[32,32]{1,0:T(8,128)}, u32[]{:S(2)}) copy-start(f32[32,32]{1,0:T(8,128)} %constant.65.clone.matrix_ref.refs_6_) | copy-start | bytes 12292
  20.2 51.8 %copy-start.3 = (f32[32,32]{1,0:T(8,128)S(1)}, f32[32,32]{1,0:T(8,128)}, u32[]{:S(2)}) copy-start(f32[32,32]{1,0:T(8,128)} %constant.66.clone.matrix_t_ref.refs_7_) | copy-start | bytes 12292
  58.9 13.0 %all-to-all-start.1 = ((f32[8,48,128]{2,1,0:T(8,128)}), f32[8,48,128]{2,1,0:T(8,128)S(1)}, u32[]{:S(2)}, u32[]{:S(2)}) async-start(f32[8,48,128]{2,1,0:T(8,128)} %shard_map.104), calls=%async_computation.1 | async-start | bytes 393216 | tf_op jit(solution)/shard_map/all_to_all | solution.py:474
  64.0 8.0 %copy-start.1 = (f32[5,32,128]{2,1,0:T(8,128)S(1)}, f32[5,32,128]{2,1,0:T(8,128)}, u32[]{:S(2)}) copy-start(f32[5,32,128]{2,1,0:T(8,128)} %constant.67.clone.table_ref.refs_8_) | copy-start | bytes 245764
  73.2 6.5 %collective-permute-start.1 = (f32[8,48,128]{2,1,0:T(8,128)S(1)}, f32[8,48,128]{2,1,0:T(8,128)S(1)}, u32[]{:S(2)}, u32[]{:S(2)}) collective-permute-start(f32[8,48,128]{2,1,0:T(8,128)S(1)} %get-tuple-element.8.refs_1_), channel_id=1, source_target_pairs={{7,0},{0,8},{8,16},{16,24},{24,28},{28,20},{20,12},{12,4},{4,1},{1... | collective-permute-start | bytes 589832 | tf_op jit(solution)/shard_map/ppermute | solution.py:505
  73.3 7.1 %collective-permute-start.2 = (f32[8,48,128]{2,1,0:T(8,128)S(1)}, f32[8,48,128]{2,1,0:T(8,128)S(1)}, u32[]{:S(2)}, u32[]{:S(2)}) collective-permute-start(f32[8,48,128]{2,1,0:T(8,128)S(1)} %get-tuple-element.8.refs_1_), channel_id=1, source_target_pairs={{8,0},{16,8},{24,16},{28,24},{20,28},{12,20},{4,12},{1,4},{9,1},{1... | collective-permute-start | bytes 589832 | tf_op jit(solution)/shard_map/ppermute | solution.py:505
  116.4 14.4 %all-to-all-start.2 = ((f32[8,96,128]{2,1,0:T(8,128)}), f32[8,96,128]{2,1,0:T(8,128)S(1)}, u32[]{:S(2)}, u32[]{:S(2)}) async-start(f32[8,96,128]{2,1,0:T(8,128)} %shard_map.106), calls=%async_computation.2 | async-start | bytes 786432 | tf_op jit(solution)/shard_map/all_to_all | solution.py:474
  130.9 6.4 %collective-permute-start.3 = (f32[10,4,512]{2,1,0:T(4,128)S(1)}, f32[10,4,512]{2,1,0:T(4,128)S(1)}, u32[]{:S(2)}, u32[]{:S(2)}) collective-permute-start(f32[10,4,512]{2,1,0:T(4,128)S(1)} %pad_maximum_fusion.1), channel_id=1, source_target_pairs={{0,1},{1,2},{2,3},{3,0},{4,5},{5,6},{6,7},{7,4},{8,9},{9,10},{10,1... | collective-permute-start | bytes 245768 | tf_op jit(solution)/shard_map/ppermute | solution.py:487
where the time goes:
time: 179 us; the launch traced here: 178 us
  Pallas kernels  117 us (65%)
  waiting for transfers between devices  27.9 us (16%)
  starting transfers between devices  22.8 us (13%)
  local copies, waits for them, and re-layouts  5.69 us (3%)
  other arithmetic  2.83 us (2%)
  between operations  2.19 us (1%)
    pallas_call x4, Pallas kernels, call(): pl.pallas_call(kernel, out_shape=[jax.ShapeDtypeStruct(shape, f32) for sh...  117 us
    all_to_all x3, waiting for transfers between devices, exchange(): lax.all_to_all(pieces, 'bead', split_axis=0, concat_axis=0, axis_index_gr...  17.3 us
    all_to_all x3, starting transfers between devices, exchange(): lax.all_to_all(pieces, 'bead', split_axis=0, concat_axis=0, axis_index_gr...  13.5 us
    ppermute x2, waiting for transfers between devices, passed(): lax.ppermute(values, 'space', [(i, (i + step) % count) for i in range(cou...  7.4 us
    ppermute x2, starting transfers between devices, passed(): lax.ppermute(values, 'space', [(i, (i + step) % count) for i in range(cou...  6.18 us
  transfers between devices with their start and end apart: 7, of which 6 were waited for; matrix products, arithmetic and copies ran while one was open for 1% of the time, Pallas kernels for 22%

commit v1 on v0

--- a/solution.py
+++ b/solution.py
@@ -82,31 +82,17 @@
     return rows + (norms + ones if own else ones + norms)
 
 
-def weigh_plain(square):
+def weigh(square):
     inverse = lax.rsqrt(square)
     decay = jnp.exp2(square * inverse * (-1.0 / (screening * math.log(2.0))))
     return decay * ((inverse * inverse) * (inverse + 1.0 / screening))
 
 
-def weigh_log(square):
-    half = lax.log(square) * (-0.5 / math.log(2.0))
-    inverse = jnp.exp2(half)
-    decay = jnp.exp2((square * inverse * (-1.0 / (screening * math.log(2.0))) + half) + half)
-    return decay * (inverse + 1.0 / screening)
-
-
-def weigh_newton(square):
-    coarse = lax.rsqrt(square.astype(bf16)).astype(f32)
-    twice = coarse * (3.0 - square * (coarse * coarse))
-    decay = jnp.exp2(square * twice * (-0.5 / (screening * math.log(2.0))))
-    return decay * ((twice * twice) * (0.125 * twice + 0.25 / screening))
-
-
 def whole_quads(beads):
     return -(-beads // QUAD) * QUAD
 
 
-def add_forces(weigh, blocks, margin, listed, offset_ref, charge_ref, coord_ref, scratch):
+def add_forces(blocks, margin, listed, offset_ref, charge_ref, coord_ref, scratch):
     rows_ref, sums_ref, far_ref, heavy_ref, near_ref, total_ref, force_ref, *buffers = scratch
     square_refs, weight_refs = buffers[:2], buffers[2:]
     beads = coord_ref.shape[1]
@@ -202,47 +188,56 @@
         base = at_frame * width + block - at_frame * frame + margin
         return [base + offset_ref[block * listed + m] for m in range(listed)], unit - block * pairs
 
-    def squares(unit, out):
-        ats, pair = places(unit)
-        far = jnp.concatenate([far_ref[at, pair // (QUAD // 2)] for at in ats], axis=0)
-        out[...] = jnp.dot(far, near_ref[unit], preferred_element_type=f32)
-
-    def weights(square_ref, out):
-        for m in range(listed):
-            for low in range(0, BLOCK, PASS):
-                weight = weigh(square_ref[m * BLOCK + low:m * BLOCK + low + PASS, :])
-                high = weight.astype(bf16)
-                row = 2 * m * BLOCK + low
-                out[row:row + PASS, :] = high
-                out[row + BLOCK:row + BLOCK + PASS, :] = (weight - high.astype(f32)).astype(bf16)
-
-    def sums(unit, weight_ref, slot):
-        ats, pair = places(unit)
-        tables = [heavy_ref[at, pair] for at in ats]
-        total = jnp.dot(
-            jnp.concatenate([t for table in tables for t in (table, table)], axis=1),
-            weight_ref[...], preferred_element_type=f32,
+    def square(ats, pair, unit, m, out):
+        far = far_ref[ats[m], pair // (QUAD // 2)]
+        out[m * BLOCK:(m + 1) * BLOCK, :] = jnp.dot(far, near_ref[unit], preferred_element_type=f32)
+
+    def weights(m, square_ref, out):
+        for low in range(0, BLOCK, PASS):
+            weight = weigh(square_ref[m * BLOCK + low:m * BLOCK + low + PASS, :])
+            high = weight.astype(bf16)
+            row = 2 * m * BLOCK + low
+            out[row:row + PASS, :] = high
+            out[row + BLOCK:row + BLOCK + PASS, :] = (weight - high.astype(f32)).astype(bf16)
+
+    def weighted(ats, pair, m, weight_ref):
+        table = heavy_ref[ats[m], pair]
+        return jnp.dot(
+            jnp.concatenate([table, table], axis=1),
+            weight_ref[2 * m * BLOCK:2 * (m + 1) * BLOCK, :], preferred_element_type=f32,
         )
+
+    def keep(total, slot):
         for i in range(2):
             cols = slice(i * BLOCK, (i + 1) * BLOCK)
             row = i * SUM_ROWS
             spot = pl.ds(pl.multiple_of((2 * slot + i) * 8, 8), 8)
             total_ref[spot, :] = total[row:row + 8, cols] + total[row + 8:row + 16, cols]
 
-    squares(0, square_refs[0])
+    def one_unit(unit, now, other):
+        after = jnp.minimum(unit + 1, units - 1)
+        before = jnp.maximum(unit - 1, 0)
+        after_ats, after_pair = places(after)
+        before_ats, before_pair = places(before)
+        total = jnp.zeros((2 * SUM_ROWS, 2 * BLOCK), f32)
+        for m in range(listed):
+            square(after_ats, after_pair, after, m, square_refs[other])
+            weights(m, square_refs[now], weight_refs[now])
+            total = total + weighted(before_ats, before_pair, m, weight_refs[other])
+        keep(total, jnp.where(unit == 0, units, unit - 1))
+
+    first_ats, first_pair = places(0)
+    for m in range(listed):
+        square(first_ats, first_pair, 0, m, square_refs[0])
 
     def two_units(step, carry):
-        unit = 2 * step
-        squares(unit + 1, square_refs[1])
-        weights(square_refs[0], weight_refs[0])
-        sums(jnp.maximum(unit - 1, 0), weight_refs[1], jnp.where(unit == 0, units, unit - 1))
-        squares(jnp.minimum(unit + 2, units - 1), square_refs[0])
-        weights(square_refs[1], weight_refs[1])
-        sums(unit, weight_refs[0], unit)
+        one_unit(2 * step, 0, 1)
+        one_unit(2 * step + 1, 1, 0)
         return carry
 
     lax.fori_loop(0, units // 2, two_units, 0)
-    sums(units - 1, weight_refs[1], units - 1)
+    last_ats, last_pair = places(units - 1)
+    keep(sum(weighted(last_ats, last_pair, m, weight_refs[1]) for m in range(listed)), units - 1)
 
     def one_block(block, carry):
         at_frame = block // frame
@@ -335,6 +330,45 @@
         coord_ref[...] = jnp.zeros(coord_ref.shape, f32)
 
 
+def message_kernel(x_ref, p_ref, noise_ref, types_ref, offsets_ref, message_ref, charge_ref, mass_ref):
+    steps = noise_ref.shape[0]
+    _, local, edge = message_ref.shape
+    types = types_ref[...]
+    charge = jnp.zeros(types.shape, f32)
+    mass = jnp.zeros(types.shape, f32)
+    for kind in range(4):
+        charge = jnp.where(types == kind, CHARGES[kind], charge)
+        mass = jnp.where(types == kind, MASSES[kind], mass)
+    charge_ref[...] = charge
+    mass_ref[...] = mass
+    for c in range(3):
+        message_ref[c] = x_ref[c, :, :edge]
+        message_ref[3 + c] = x_ref[c, :, edge:2 * edge]
+        message_ref[6 + c] = p_ref[c, :, :edge]
+        for step in range(steps):
+            message_ref[9 + 3 * step + c] = noise_ref[step, c, :, :edge]
+    at = 9 + 3 * steps
+    for i, row in enumerate([charge[:, :edge], charge[:, edge:2 * edge], mass[:, :edge], offsets_ref[...]]):
+        message_ref[at + i] = jnp.broadcast_to(row, (local, edge))
+
+
+def pack_kernel(blocks, x_ref, noise_ref, message_ref, out_ref):
+    steps = noise_ref.shape[0]
+    _, local, edge = message_ref.shape
+    atoms = x_ref.shape[2]
+    for c in range(3 + 3 * steps):
+        for block in range(atoms // BLOCK):
+            at = edge + block * BLOCK
+            if at >= atoms:
+                value = message_ref[c if c < 3 else 6 + c, :, at - atoms:at - atoms + BLOCK]
+            elif c < 3:
+                value = x_ref[c, :, at:at + BLOCK]
+            else:
+                value = noise_ref[c // 3 - 1, c % 3, :, at:at + BLOCK]
+            row = row_of(c, block % blocks, blocks, local)
+            out_ref[block // blocks, row:row + local, :] = value
+
+
 def first_kernel(
     shares, margin, listed, offset_ref, charge_ref, x_ref, message_ref, p_ref, pout_ref, coord_ref, *scratch
 ):
@@ -347,7 +381,7 @@
         coord_ref[c, :local, 0:atoms] = x_ref[c]
         for part in range(2):
             coord_ref[c, :local, atoms + part * edge:atoms + (part + 1) * edge] = message_ref[3 * part + c]
-    add_forces(weigh_log, blocks, margin, listed, offset_ref, charge_ref, coord_ref, scratch)
+    add_forces(blocks, margin, listed, offset_ref, charge_ref, coord_ref, scratch)
     force_ref = scratch[FORCE]
     for c in range(3):
         for block in range(blocks):
@@ -382,7 +416,7 @@
             at = 2 * edge + block * BLOCK
             coord_ref[c, :local, at:at + BLOCK] = taken(c, block)
         xout_ref[c] = coord_ref[c, :local, edge:edge + atoms]
-    add_forces(weigh_newton, blocks, margin, listed, offset_ref, charge_ref, coord_ref, scratch)
+    add_forces(blocks, margin, listed, offset_ref, charge_ref, coord_ref, scratch)
     force_ref = scratch[FORCE]
     for c in range(3):
         for block in range(blocks):
@@ -441,7 +475,7 @@
     width = blocks * BLOCK
     for part in range(parts):
         unpack_beads(x_refs[part], 0, blocks, local, coord_ref, part * width)
-    add_forces(weigh_plain, blocks, hops * blocks, listed, offset_ref, charge_ref, coord_ref, scratch)
+    add_forces(blocks, hops * blocks, listed, offset_ref, charge_ref, coord_ref, scratch)
     force_ref = scratch[FORCE]
     unpack_beads(p_ref, 0, blocks, local, coord_ref, 0)
     unpack_beads(noise_ref, noise_base, blocks, local, coord_ref, (parts - 1) * width)
@@ -472,14 +506,6 @@
     order = fold(pieces.shape[0])
     group = [order.index(at) for at in range(len(order))]
     return lax.all_to_all(pieces, "bead", split_axis=0, concat_axis=0, axis_index_groups=[group], tiled=True)
-
-
-def pack_shares(values):
-    count = lax.axis_size("bead")
-    lead, local, atoms = values.shape
-    blocks = atoms // (count * BLOCK)
-    pieces = values.reshape(lead, local, count, blocks, BLOCK).transpose(2, 0, 3, 1, 4)
-    return pieces.reshape(count, lead * blocks * local, BLOCK)
 
 
 def passed(values, step):
@@ -520,31 +546,24 @@
     listed = neighbours.shape[1]
     order = fold(count)
 
-    charge = jnp.zeros(atom_types.shape, f32)
-    mass = jnp.zeros(atom_types.shape, f32)
-    for kind in range(4):
-        charge = jnp.where(atom_types == kind, CHARGES[kind], charge)
-        mass = jnp.where(atom_types == kind, MASSES[kind], mass)
     own = lax.axis_index("space") * domain + jnp.arange(domain, dtype=jnp.int32)
-    offsets = jnp.clip(neighbours - own[:, None], -margin, margin)
-    noises = thermal_noise.reshape(3 * steps, local, atoms)
-
-    wide = jnp.stack([
-        charge[:edge], charge[edge:2 * edge], mass[:edge],
-        jnp.pad(offsets[:margin].astype(f32).reshape(-1), (0, edge - margin * listed)),
-    ])
-    message = passed(jnp.concatenate([
-        positions[:, :, :edge], positions[:, :, edge:2 * edge], momenta[:, :, :edge], noises[:, :, :edge],
-        jnp.broadcast_to(wide[:, None, :], (4, local, edge)),
-    ], axis=0), -1)
+    offsets = jnp.clip(neighbours - own[:, None], -margin, margin).reshape(-1)
+    sent = jnp.pad(offsets[:margin * listed].astype(f32), (0, edge - margin * listed))[None, :]
+
+    message, charge, mass = call(
+        message_kernel, (positions, momenta, thermal_noise, atom_types[None, :], sent), 0,
+        [(13 + 3 * steps, local, edge), (1, atoms), (1, atoms)], [], 0,
+    )
+    message = passed(message, -1)
     side = message[9 + 3 * steps:, 0]
-    first_charge = jnp.concatenate([charge, side[0], side[1]])[None, :]
-    moved_mass = jnp.concatenate([mass[edge:], side[2]])
-    moved_offsets = jnp.concatenate([offsets[margin:].reshape(-1), side[3, :margin * listed].astype(jnp.int32)])
-    rest = exchange(pack_shares(jnp.concatenate([
-        jnp.concatenate([positions, noises], axis=0)[:, :, edge:],
-        jnp.concatenate([message[:3], message[9:9 + 3 * steps]], axis=0),
-    ], axis=2)))
+    first_charge = jnp.concatenate([charge, side[:1], side[1:2]], axis=1)
+    moved_mass = jnp.concatenate([mass[0, edge:], side[2]])
+    moved_offsets = jnp.concatenate([offsets[margin * listed:], side[3, :margin * listed].astype(jnp.int32)])
+    (rest,) = call(
+        functools.partial(pack_kernel, blocks), (positions, thermal_noise, message), 0,
+        [(count, (3 + 3 * steps) * blocks * local, BLOCK)], [], 0,
+    )
+    rest = exchange(rest)
 
     place = jnp.asarray(np.array(order, np.int32))[lax.axis_index("bead")]
     near_charge = lax.dynamic_slice_in_dim(first_charge, place * share, share + 2 * edge, axis=1)
@@ -586,11 +605,11 @@
 
     message = passed(jnp.concatenate([
         ends(count - 2 * hops, 0), ends(count - hops, 0), ends(count - hops, 1),
-        jnp.broadcast_to(charge[None, None, atoms - edge:], (1, local, edge)),
+        jnp.broadcast_to(charge[:, None, atoms - edge:], (1, local, edge)),
     ], axis=0), 1)
     last_charge = jnp.concatenate([message[9, 0], first_charge[0, :atoms + edge]])[None, :]
     return tuple(call(
-        functools.partial(last_kernel, margin, listed), (offsets.reshape(-1), last_charge, both, message), 1,
+        functools.partial(last_kernel, margin, listed), (offsets, last_charge, both, message), 1,
         [(3, local, atoms)] * 2, force_scratch(local, domain, margin, listed), pairs,
     ))
 

time: 179 us -> 163 us (0.911)
  Pallas kernels: 117 us -> 104 us
  other arithmetic: 2.83 us -> 0.28 us
    pallas_call x4 -> x6, Pallas kernels: 117 us -> 104 us  [call(): pl.pallas_call(kernel, out_shape=[jax.ShapeDtypeStruct(shape, f32) for sh...]
    reshape x5 -> x1, local copies, waits for them, and re-layouts: 1.99 us -> 0.1 us  [body(): offsets = jnp.clip(neighbours - own[:, None], -margin, margin).reshape(-1)]
    unnamed x17 -> x25, local copies, waits for them, and re-layouts: 2.38 us -> 4.07 us
  transfers between devices with their start and end apart: 7 -> 7, of which waited for: 6 -> 6; matrix products, arithmetic and copies ran while one was open for 1% -> 1% of each run, Pallas kernels for 22% -> 20%
where the time goes in v1:
time: 163 us
  Pallas kernels  104 us (64%)
  waiting for transfers between devices  27.6 us (17%)
  starting transfers between devices  23 us (14%)
  local copies, waits for them, and re-layouts  5.55 us (3%)
  between operations  2.14 us (1%)
    pallas_call x6, Pallas kernels, call(): pl.pallas_call(kernel, out_shape=[jax.ShapeDtypeStruct(shape, f32) for sh...  104 us
    all_to_all x3, waiting for transfers between devices, exchange(): lax.all_to_all(pieces, 'bead', split_axis=0, concat_axis=0, axis_index_gr...  16.7 us
    all_to_all x3, starting transfers between devices, exchange(): lax.all_to_all(pieces, 'bead', split_axis=0, concat_axis=0, axis_index_gr...  13.6 us
    ppermute x2, waiting for transfers between devices, passed(): lax.ppermute(values, 'space', [(i, (i + step) % count) for i in range(cou...  6.92 us
    ppermute x2, starting transfers between devices, passed(): lax.ppermute(values, 'space', [(i, (i + step) % count) for i in range(cou...  6.19 us
    unnamed x25, local copies, waits for them, and re-layouts  4.07 us
    ppermute x2, waiting for transfers between devices, window(): out.append(lax.ppermute(values, ('bead', 'space'), route))  3.98 us
  transfers between devices with their start and end apart: 7, of which 6 were waited for; matrix products, arithmetic and copies ran while one was open for 1% of the time, Pallas kernels for 20%

profile of v1, /device:TPU:0, one launch (start us, length us, event | category | flops | bytes accessed | tf_op | source)
XLA Modules:
  0.0 162.8 jit_solution(5345917301582587742)
XLA Ops:
  0.6 0.0 copy-start.10
  0.7 0.7 copy-done.10
  1.3 0.0 copy-start.9
  1.3 0.1 copy.17
  1.4 0.1 convert_element_type.15
  1.5 0.5 copy-done.9
  2.0 1.0 copy-done
  3.0 0.9 copy-done.2
  4.0 0.9 copy-done.4
  4.9 3.9 %collective-permute-start = (f32[19,4,512]{2,1,0:T(4,128)S(1)}, f32[19,4,512]{2,1,0:T(4,128)S(1)}, u32[]{:S(2)}, u32[]{:S(2)}) collective-permute-start(f32[19,4,512]{2,1,0:T(4,128)S(1)} %get-tuple-element.9), channel_id=1, source_target_pairs={{0,3},{1,0},{2,1},{3,2},{4,7},{5,4},{6,5},{7,6},{8,11},{9,8},{10,9... | collective-permute-start | bytes 466952 | tf_op jit(solution)/shard_map/ppermute | solution.py:513
  8.9 0.1 slice.55
  8.9 0.1 copy.16
  9.0 0.1 slice.56
  9.1 3.0 %collective-permute-done.message_ref = f32[19,4,512]{2,1,0:T(4,128)S(1)} collective-permute-done((f32[19,4,512]{2,1,0:T(4,128)S(1)}, f32[19,4,512]{2,1,0:T(4,128)S(1)}, u32[]{:S(2)}, u32[]{:S(2)}) %collective-permute-start) | collective-permute-done | bytes 155680 | tf_op jit(solution)/shard_map/ppermute | solution.py:513
  12.2 0.0 copy-done.1
  12.2 0.0 copy-done.3
  12.2 0.9 shard_map.106
  13.0 5.0 %all-to-all-start = ((f32[8,144,128]{2,1,0:T(8,128)}), f32[8,144,128]{2,1,0:T(8,128)S(1)}, u32[]{:S(2)}, u32[]{:S(2)}) async-start(f32[8,144,128]{2,1,0:T(8,128)} %shard_map.106), calls=%async_computation | async-start | bytes 1179648 | tf_op jit(solution)/shard_map/all_to_all | solution.py:508
  18.1 0.1 pad_add_fusion.offset_ref
  18.2 0.0 copy-done.5
  18.2 0.0 copy-start.11
  18.2 0.0 copy-start.8
  18.2 32.7 %shard_map.105 = f32[8,48,128]{2,1,0:T(8,128)} custom-call(s32[160]{0:T(256)S(1)} %pad_add_fusion.offset_ref, f32[1,5120]{1,0:T(1,128)S(1)} %pad_maximum_fusion.1.charge_ref, f32[3,4,4096]{2,1,0:T(4,128)S(1)} %copy-done.3, f32[19,4,512]{2,1,0:T(4,128)S(1)} %collective-permute-done.message_ref, f32[3,4,4096]{2,1,0:T(4,128)S(1)} %copy-done.5), custom_call_target="tpu_custom_call" | custom-call | flops 209716224 | bytes 4194304 | tf_op jit(solution)/shard_map/pallas_call | solution.py:290
  50.9 0.0 all-to-all-done.rest_ref.refs_4_
  50.9 5.1 %all-to-all-start.1 = ((f32[8,48,128]{2,1,0:T(8,128)}), f32[8,48,128]{2,1,0:T(8,128)S(1)}, u32[]{:S(2)}, u32[]{:S(2)}) async-start(f32[8,48,128]{2,1,0:T(8,128)} %shard_map.105), calls=%async_computation.1 | async-start | bytes 393216 | tf_op jit(solution)/shard_map/all_to_all | solution.py:508
  56.0 0.0 copy-done.11
  56.0 0.6 dynamic_slice.12
  58.0 0.0 copy-start.7
  58.0 0.1 dynamic_slice.13.offset_ref
  58.1 0.1 fusion
  58.1 5.8 %all-to-all-done.1.p_ref = f32[8,48,128]{2,1,0:T(8,128)S(1)} async-done(((f32[8,48,128]{2,1,0:T(8,128)}), f32[8,48,128]{2,1,0:T(8,128)S(1)}, u32[]{:S(2)}, u32[]{:S(2)}) %all-to-all-start.1) | async-done | bytes 196640 | tf_op jit(solution)/shard_map/all_to_all | solution.py:508
  64.0 0.0 copy-done.8
  64.0 0.0 copy-done.6
  64.0 0.0 copy-done.7
  64.0 1.2 shard_map.107
  65.2 0.1 collective-permute-start.1
  65.3 3.1 %collective-permute-start.2 = (f32[8,48,128]{2,1,0:T(8,128)S(1)}, f32[8,48,128]{2,1,0:T(8,128)S(1)}, u32[]{:S(2)}, u32[]{:S(2)}) collective-permute-start(f32[8,48,128]{2,1,0:T(8,128)S(1)} %get-tuple-element.14.refs_1_), channel_id=1, source_target_pairs={{8,0},{16,8},{24,16},{28,24},{20,28},{12,20},{4,12},{1,4},{9,1},{1... | collective-permute-start | bytes 589832 | tf_op jit(solution)/shard_map/ppermute | solution.py:531
  68.4 3.3 %collective-permute-done.1.refs_0_ = f32[8,48,128]{2,1,0:T(8,128)S(1)} collective-permute-done((f32[8,48,128]{2,1,0:T(8,128)S(1)}, f32[8,48,128]{2,1,0:T(8,128)S(1)}, u32[]{:S(2)}, u32[]{:S(2)}) %collective-permute-start.1) | collective-permute-done | bytes 196640 | tf_op jit(solution)/shard_map/ppermute | solution.py:531
  71.7 0.7 collective-permute-done.2.refs_2_
  72.4 36.7 %shard_map.108 = f32[8,96,128]{2,1,0:T(8,128)} custom-call(s32[20]{0:T(128)S(1)} %dynamic_slice.13.offset_ref, f32[1,1536]{1,0:T(1,128)S(1)} %constant_dynamic-slice_fusion.charge_ref, f32[8,48,128]{2,1,0:T(8,128)S(1)} %collective-permute-done.1.refs_0_, f32[8,48,128]{2,1,0:T(8,128)S(1)} %get-tuple-element.14.refs_1_, ...), custom_call_target="tpu_custom_call" | custom-call | flops 209716224 | bytes 4194304 | tf_op jit(solution)/shard_map/pallas_call | solution.py:290
  109.1 3.5 %all-to-all-start.2 = ((f32[8,96,128]{2,1,0:T(8,128)}), f32[8,96,128]{2,1,0:T(8,128)S(1)}, u32[]{:S(2)}, u32[]{:S(2)}) async-start(f32[8,96,128]{2,1,0:T(8,128)} %shard_map.108), calls=%async_computation.2 | async-start | bytes 786432 | tf_op jit(solution)/shard_map/all_to_all | solution.py:508
  112.6 10.9 %all-to-all-done.2.both_ref = f32[8,96,128]{2,1,0:T(8,128)S(1)} async-done(((f32[8,96,128]{2,1,0:T(8,128)}), f32[8,96,128]{2,1,0:T(8,128)S(1)}, u32[]{:S(2)}, u32[]{:S(2)}) %all-to-all-start.2) | async-done | bytes 393248 | tf_op jit(solution)/shard_map/all_to_all | solution.py:508
  123.7 2.2 %collective-permute-start.3 = (f32[10,4,512]{2,1,0:T(4,128)S(1)}, f32[10,4,512]{2,1,0:T(4,128)S(1)}, u32[]{:S(2)}, u32[]{:S(2)}) collective-permute-start(f32[10,4,512]{2,1,0:T(4,128)S(1)} %pad_maximum_fusion), channel_id=1, source_target_pairs={{0,1},{1,2},{2,3},{3,0},{4,5},{5,6},{6,7},{7,4},{8,9},{9,10},{10,1... | collective-permute-start | bytes 245768 | tf_op jit(solution)/shard_map/ppermute | solution.py:513
  125.9 0.1 copy.15
  126.0 0.1 reshape.44.offset_ref
  126.1 0.1 maximum_reduce_fusion
  126.2 3.9 %collective-permute-done.3.message_ref = f32[10,4,512]{2,1,0:T(4,128)S(1)} collective-permute-done((f32[10,4,512]{2,1,0:T(4,128)S(1)}, f32[10,4,512]{2,1,0:T(4,128)S(1)}, u32[]{:S(2)}, u32[]{:S(2)}) %collective-permute-start.3) | collective-permute-done | bytes 81952 | tf_op jit(solution)/shard_map/ppermute | solution.py:513
  130.1 32.7 %shard_map.109 = (f32[3,4,4096]{2,1,0:T(4,128)}, f32[3,4,4096]{2,1,0:T(4,128)}) custom-call(s32[160]{0:T(256)S(1)} %reshape.44.offset_ref, f32[1,5120]{1,0:T(1,128)S(1)} %bitcast.36, f32[8,96,128]{2,1,0:T(8,128)S(1)} %all-to-all-done.2.both_ref, f32[10,4,512]{2,1,0:T(4,128)S(1)} %collective-permute-done.3.message_ref), custom_call_target="tpu_custom_call" | custom-call | flops 209716224 | bytes 4194304 | tf_op jit(solution)/shard_map/pallas_call | solution.py:290
  (31 shorter events, 0.3 us)
Async XLA Ops:
  0.6 0.7 copy-start.10
  1.3 0.7 copy-start.9
  2.0 1.0 copy-start
  3.0 0.9 copy-start.2
  4.0 0.9 copy-start.4
  4.9 7.3 %copy-start.1 = (f32[2,3,4,4096]{3,2,1,0:T(4,128)S(1)}, f32[2,3,4,4096]{3,2,1,0:T(4,128)}, u32[]{:S(2)}) copy-start(f32[2,3,4,4096]{3,2,1,0:T(4,128)} %noise_ref.3) | copy-start | bytes 1179652
  4.9 7.3 %copy-start.3 = (f32[3,4,4096]{2,1,0:T(4,128)S(1)}, f32[3,4,4096]{2,1,0:T(4,128)}, u32[]{:S(2)}) copy-start(f32[3,4,4096]{2,1,0:T(4,128)} %x_ref.5) | copy-start | bytes 589828
  4.9 7.2 %collective-permute-start = (f32[19,4,512]{2,1,0:T(4,128)S(1)}, f32[19,4,512]{2,1,0:T(4,128)S(1)}, u32[]{:S(2)}, u32[]{:S(2)}) collective-permute-start(f32[19,4,512]{2,1,0:T(4,128)S(1)} %get-tuple-element.9), channel_id=1, source_target_pairs={{0,3},{1,0},{2,1},{3,2},{4,7},{5,4},{6,5},{7,6},{8,11},{9,8},{10,9... | collective-permute-start | bytes 466952 | tf_op jit(solution)/shard_map/ppermute | solution.py:513
  13.0 5.2 %copy-start.5 = (f32[3,4,4096]{2,1,0:T(4,128)S(1)}, f32[3,4,4096]{2,1,0:T(4,128)}, u32[]{:S(2)}) copy-start(f32[3,4,4096]{2,1,0:T(4,128)} %p_ref.3) | copy-start | bytes 589828
  13.0 37.9 %all-to-all-start = ((f32[8,144,128]{2,1,0:T(8,128)}), f32[8,144,128]{2,1,0:T(8,128)S(1)}, u32[]{:S(2)}, u32[]{:S(2)}) async-start(f32[8,144,128]{2,1,0:T(8,128)} %shard_map.106), calls=%async_computation | async-start | bytes 1179648 | tf_op jit(solution)/shard_map/all_to_all | solution.py:508
  18.2 37.8 %copy-start.11 = (s32[8]{0:T(128)S(1)}, s32[8]{0:T(128)}, u32[]{:S(2)}) copy-start(s32[8]{0:T(128)} %constant.42.clone) | copy-start | bytes 100
  18.2 45.7 %copy-start.8 = (f32[32,32]{1,0:T(8,128)S(1)}, f32[32,32]{1,0:T(8,128)}, u32[]{:S(2)}) copy-start(f32[32,32]{1,0:T(8,128)} %constant.44.clone.matrix_t_ref.refs_7_) | copy-start | bytes 12292
  50.9 13.1 %all-to-all-start.1 = ((f32[8,48,128]{2,1,0:T(8,128)}), f32[8,48,128]{2,1,0:T(8,128)S(1)}, u32[]{:S(2)}, u32[]{:S(2)}) async-start(f32[8,48,128]{2,1,0:T(8,128)} %shard_map.105), calls=%async_computation.1 | async-start | bytes 393216 | tf_op jit(solution)/shard_map/all_to_all | solution.py:508
  56.0 8.0 %copy-start.6 = (f32[5,32,128]{2,1,0:T(8,128)S(1)}, f32[5,32,128]{2,1,0:T(8,128)}, u32[]{:S(2)}) copy-start(f32[5,32,128]{2,1,0:T(8,128)} %constant.45.clone.table_ref.refs_8_) | copy-start | bytes 245764
  58.0 6.0 %copy-start.7 = (f32[32,32]{1,0:T(8,128)S(1)}, f32[32,32]{1,0:T(8,128)}, u32[]{:S(2)}) copy-start(f32[32,32]{1,0:T(8,128)} %constant.43.clone.matrix_ref.refs_6_) | copy-start | bytes 12292
  65.2 6.5 %collective-permute-start.1 = (f32[8,48,128]{2,1,0:T(8,128)S(1)}, f32[8,48,128]{2,1,0:T(8,128)S(1)}, u32[]{:S(2)}, u32[]{:S(2)}) collective-permute-start(f32[8,48,128]{2,1,0:T(8,128)S(1)} %get-tuple-element.14.refs_1_), channel_id=1, source_target_pairs={{7,0},{0,8},{8,16},{16,24},{24,28},{28,20},{20,12},{12,4},{4,1},{1... | collective-permute-start | bytes 589832 | tf_op jit(solution)/shard_map/ppermute | solution.py:531
  65.3 7.1 %collective-permute-start.2 = (f32[8,48,128]{2,1,0:T(8,128)S(1)}, f32[8,48,128]{2,1,0:T(8,128)S(1)}, u32[]{:S(2)}, u32[]{:S(2)}) collective-permute-start(f32[8,48,128]{2,1,0:T(8,128)S(1)} %get-tuple-element.14.refs_1_), channel_id=1, source_target_pairs={{8,0},{16,8},{24,16},{28,24},{20,28},{12,20},{4,12},{1,4},{9,1},{1... | collective-permute-start | bytes 589832 | tf_op jit(solution)/shard_map/ppermute | solution.py:531
  109.1 14.4 %all-to-all-start.2 = ((f32[8,96,128]{2,1,0:T(8,128)}), f32[8,96,128]{2,1,0:T(8,128)S(1)}, u32[]{:S(2)}, u32[]{:S(2)}) async-start(f32[8,96,128]{2,1,0:T(8,128)} %shard_map.108), calls=%async_computation.2 | async-start | bytes 786432 | tf_op jit(solution)/shard_map/all_to_all | solution.py:508
  123.7 6.4 %collective-permute-start.3 = (f32[10,4,512]{2,1,0:T(4,128)S(1)}, f32[10,4,512]{2,1,0:T(4,128)S(1)}, u32[]{:S(2)}, u32[]{:S(2)}) collective-permute-start(f32[10,4,512]{2,1,0:T(4,128)S(1)} %pad_maximum_fusion), channel_id=1, source_target_pairs={{0,1},{1,2},{2,3},{3,0},{4,5},{5,6},{6,7},{7,4},{8,9},{9,10},{10,1... | collective-permute-start | bytes 245768 | tf_op jit(solution)/shard_map/ppermute | solution.py:513
